TPU v7x, 512 devices: a whole 4x8x8 slice. The times are simulated.
512 devices in a mesh: stem: 8 (over x, y_hi), tm: 64 (over z, y_lo, core).
Axes of the slice: x: 4, y: 8 (y_hi: 2, y_lo: 4; y = y_hi * 4 + y_lo), z: 8, core: 2. Of those that a mesh axis runs over, the one named last changes fastest.
Arguments:
- hidden: bfloat16 [8, 4096, 1024], P('stem', 'tm'), may hold values from -3 to 3
- control_ids: int32 [4096], P('tm'), may hold values from 0 to 127
- control_table: bfloat16 [128, 1024], replicated, may hold values from -3 to 3
- activity: int32 [8, 32], P('stem'), may hold values from 0 to 1, as said below
- ada: float32 [8, 3, 1024], P('stem'), may hold values from -4 to 4
- w_qkv: bfloat16 [1024, 1536], replicated, may hold values from -1 to 1
- w_out: bfloat16 [512, 1024], replicated, may hold values from -0.25 to 0.25
Outputs:
- block_out: bfloat16 [8, 4096, 1024], P('stem', 'tm')
Inputs may be any that keep to these rules, and one draw needn't show every extreme that they name: `activity`: 1 marks an active bar of a stem, 0 a silent one.
All inputs are finite; a program needn't handle non-finite values.
Results may differ from a plain program's by a relative error of at most 0.019.
Values may be sent and summed in bfloat16 or wider, within the bound.
A program may use at most 64 MiB of HBM per device.

v0:
```python
import math

import jax
import jax.numpy as jnp
from jax import lax
from jax.sharding import PartitionSpec as P

HEADS = 8
HEAD_DIM = 64
BAR = 128


epsilon = 1e-06


def bar_live(frame_ids, activity_row):
    bar_count = activity_row.shape[0]
    hits = frame_ids[:, None] // BAR == jnp.arange(bar_count, dtype=jnp.int32)[None, :]
    return jnp.sum(jnp.where(hits, activity_row[None, :], 0), axis=1) > 0


def stem_state(queries, key_all, value_all, score_scale):
    scores = (
        jnp.einsum("qhd,sqhd->qhs", queries, key_all, preferred_element_type=jnp.float32)
        * score_scale
    )
    row_max = jnp.max(scores, axis=-1)
    weights = jnp.exp(scores - row_max[..., None])
    numerator = jnp.einsum(
        "qhs,sqhd->qhd", weights.astype(jnp.bfloat16), value_all, preferred_element_type=jnp.float32
    )
    return (row_max, jnp.sum(weights, axis=-1), numerator)


def block_size(count):
    for candidate in range(min(count, 512), 0, -1):
        if count % candidate == 0:
            return candidate
    return count


def body(hidden, control_ids, control_table, activity, ada, w_qkv, w_out):
    frames = hidden.shape[1]
    inner_width = w_out.shape[0]
    head_count = HEADS
    head_dim = HEAD_DIM
    vocabulary = control_table.shape[0]
    score_scale = 1.0 / math.sqrt(head_dim)
    one_hot = (control_ids[:, None] == jnp.arange(vocabulary, dtype=jnp.int32)[None, :]).astype(
        jnp.bfloat16
    )
    lookup = jnp.dot(one_hot, control_table, preferred_element_type=jnp.float32)
    residual = hidden[0].astype(jnp.float32) + lookup
    row_mean = jnp.mean(residual, axis=-1, keepdims=True)
    row_var = jnp.mean(jnp.square(residual - row_mean), axis=-1, keepdims=True)
    normed = (
        (residual - row_mean) * lax.rsqrt(row_var + epsilon) * (1.0 + ada[0, 1]) + ada[0, 0]
    ).astype(jnp.bfloat16)
    projected = jnp.dot(normed, w_qkv, preferred_element_type=jnp.float32).astype(jnp.bfloat16)
    queries = projected[:, :inner_width].reshape(frames, head_count, head_dim)
    key_rows = projected[:, inner_width : 2 * inner_width]
    value_rows = projected[:, 2 * inner_width :]
    gathered = (
        lax.all_gather(key_rows[None], "stem", axis=0, tiled=True),
        lax.all_gather(value_rows[None], "stem", axis=0, tiled=True),
    )
    key_all = gathered[0].reshape(-1, frames, head_count, head_dim)
    value_all = gathered[1].reshape(-1, frames, head_count, head_dim)
    running = stem_state(queries, key_all, value_all, score_scale)
    activity_row = activity[0]
    own_frames = lax.axis_index("tm") * frames + jnp.arange(frames, dtype=jnp.int32)
    own_live = bar_live(own_frames, activity_row)

    def merge_block(state_now, key_block, value_block, offset):
        key_frames = offset + jnp.arange(key_block.shape[0], dtype=jnp.int32)
        allowed = (
            own_live[:, None]
            & bar_live(key_frames, activity_row)[None, :]
            & (own_frames[:, None] != key_frames[None, :])
        )
        old_max, old_total, old_numerator = state_now
        scores = (
            jnp.einsum("qhd,khd->qhk", queries, key_block, preferred_element_type=jnp.float32)
            * score_scale
        )
        scores = jnp.where(allowed[:, None, :], scores, -1e30)
        new_max = jnp.maximum(old_max, jnp.max(scores, axis=-1))
        rescale = jnp.exp(old_max - new_max)
        weights = jnp.exp(scores - new_max[..., None])
        new_total = old_total * rescale + jnp.sum(weights, axis=-1)
        new_numerator = old_numerator * rescale[..., None] + jnp.einsum(
            "qhk,khd->qhd",
            weights.astype(jnp.bfloat16),
            value_block,
            preferred_element_type=jnp.float32,
        )
        return (new_max, new_total, new_numerator)

    key_piece = lax.all_gather(key_rows, "tm", axis=0, tiled=True)
    value_piece = lax.all_gather(value_rows, "tm", axis=0, tiled=True)
    count = key_piece.shape[0]
    block_len = block_size(count)
    block_count = count // block_len
    key_blocks = key_piece.reshape(block_count, block_len, head_count, head_dim)
    value_blocks = value_piece.reshape(block_count, block_len, head_count, head_dim)
    offsets = jnp.int32(0) + block_len * jnp.arange(block_count, dtype=jnp.int32)

    def advance(state_inner, block_item):
        return (merge_block(state_inner, block_item[0], block_item[1], block_item[2]), None)

    state_out, unused = lax.scan(advance, running, (key_blocks, value_blocks, offsets))
    final_max, final_total, final_numerator = state_out
    attended = (
        (final_numerator / final_total[..., None]).astype(jnp.bfloat16).reshape(frames, inner_width)
    )
    branch = jnp.dot(attended, w_out, preferred_element_type=jnp.float32)
    return (residual + ada[0, 2] * branch).astype(jnp.bfloat16)[None]


def solution(mesh):
    placed = (P("stem", "tm", None), P("tm"), P(), P("stem", None), P("stem", None, None), P(), P())
    return jax.shard_map(
        body, mesh=mesh, in_specs=placed, out_specs=P("stem", "tm", None), check_vma=False
    )
```

profile of v0, /device:TPU:1, one launch (start us, length us, event | category | flops | bytes accessed | tf_op | source)
XLA Modules:
  0.0 343.0 jit_solution(14053732741011831266)
XLA Ops:
  6.5 1.5 fusion.35
  12.8 47.3 %all-gather = bf16[512,512]{1,0:T(8,128)(2,1)} all-gather(bf16[64,512]{1,0:T(8,128)(2,1)} %get-tuple-element.233), channel_id=2, replica_groups=mesh['stem'=8,'tm'=64] {'stem'}, dimensions={0}, use_global_device_ids=true | all-gather | bytes 589824 | tf_op jit(solution)/shard_map/all_gather | solution.py:64
  60.1 2.4 reshape.178
  62.5 2.2 fusion.21
  65.1 49.2 %all-gather.1 = bf16[512,512]{1,0:T(8,128)(2,1)} all-gather(bf16[64,512]{1,0:T(8,128)(2,1)S(1)} %copy-done.2), channel_id=3, replica_groups=mesh['stem'=8,'tm'=64] {'stem'}, dimensions={0}, use_global_device_ids=true | all-gather | bytes 589824 | tf_op jit(solution)/shard_map/all_gather | solution.py:65
  114.3 2.4 reshape.179
  116.7 2.5 multiply_reduce_fusion
  121.9 21.6 %all-gather.5.cloned.1.call-done = bf16[4096,512]{1,0:T(8,128)(2,1)} async-done(((bf16[64,512]{1,0:T(8,128)(2,1)}), bf16[4096,512]{1,0:T(8,128)(2,1)}) %all-gather.5.cloned.1.call-update) | async-done | bytes 4194320 | tf_op jit(solution)/shard_map/all_gather | solution.py:99
  143.5 11.2 %reshape.194 = bf16[8,512,8,64]{3,2,1,0:T(8,128)(2,1)} reshape(bf16[4096,512]{1,0:T(8,128)(2,1)} %all-gather.5.cloned.1.call-done) | data formatting | bytes 8388608 | tf_op jit(solution)/shard_map/reshape | solution.py:104
  154.7 9.8 %copy.20 = bf16[8,512,8,64]{1,3,2,0:T(8,128)(2,1)} copy(bf16[8,512,8,64]{3,2,1,0:T(8,128)(2,1)} %reshape.194) | data formatting | bytes 8388608
  164.4 99.9 %all-gather.7.cloned.1.call-done = bf16[4096,512]{1,0:T(8,128)(2,1)} async-done(((bf16[64,512]{1,0:T(8,128)(2,1)}), bf16[4096,512]{1,0:T(8,128)(2,1)}) %all-gather.7.cloned.1.call-update) | async-done | bytes 4194320 | tf_op jit(solution)/shard_map/all_gather | solution.py:100
  264.4 11.2 %reshape.195 = bf16[8,512,8,64]{3,2,1,0:T(8,128)(2,1)} reshape(bf16[4096,512]{1,0:T(8,128)(2,1)} %all-gather.7.cloned.1.call-done) | data formatting | bytes 8388608 | tf_op jit(solution)/shard_map/reshape | solution.py:105
  275.5 9.7 %copy.22 = bf16[8,512,8,64]{1,3,2,0:T(8,128)(2,1)} copy(bf16[8,512,8,64]{3,2,1,0:T(8,128)(2,1)} %reshape.195) | data formatting | bytes 8388608
  285.3 48.6 %while.17 = (s32[]{:T(128)}, f32[64,8]{0,1:T(8,128)S(1)}, f32[64,8]{0,1:T(8,128)S(1)}, f32[64,8,64]{0,2,1:T(8,128)S(1)}, pred[64]{0:T(512)(128)(4,1)S(1)}, /*ind...) while((s32[]{:T(128)}, f32[64,8]{0,1:T(8,128)S(1)}, ...), condition=%wide.region_9.10_spmd.clone, body=%wide.region_5.9_spmd.clone.sunk | while | flops 69166144 | bytes 4635465 | solution.py:111
  288.1 1.4 fusion.51
  289.9 1.5 fusion.53
  294.1 1.4 fusion.51
  295.9 1.5 fusion.53
  300.2 1.4 fusion.51
  302.0 1.5 fusion.53
  303.5 1.3 dynamic_slice.38
  306.3 1.4 fusion.51
  308.1 1.5 fusion.53
  312.4 1.4 fusion.51
  314.1 1.5 fusion.53
  318.4 1.4 fusion.51
  320.2 1.5 fusion.53
  324.5 1.4 fusion.51
  326.3 1.5 fusion.53
  330.6 1.4 fusion.51
  332.4 1.5 fusion.53
  333.9 2.2 fusion.20
  (110 shorter events, 31.7 us)
Async XLA Ops:
  6.5 2.5 copy-start
  6.5 137.0 %all-gather.5.cloned.1.call-start = ((), (), s32[]{:S(2)}) async-start(), calls=%async_computation | async-start | bytes 4259840 | tf_op jit(solution)/shard_map/all_gather | solution.py:99
  8.0 1.0 copy-start.1
  10.4 54.7 %copy-start.2 = (bf16[64,512]{1,0:T(8,128)(2,1)S(1)}, bf16[64,512]{1,0:T(8,128)(2,1)}, u32[]{:S(2)}) copy-start(bf16[64,512]{1,0:T(8,128)(2,1)} %get-tuple-element.232) | copy-start | bytes 196612
  10.4 254.0 %all-gather.7.cloned.1.call-start = ((), (), s32[]{:S(2)}) async-start(), calls=%async_computation.1 | async-start | bytes 4259840 | tf_op jit(solution)/shard_map/all_gather | solution.py:100
  60.1 61.6 %copy-start.3 = (s32[1,32]{1,0:T(1,128)S(1)}, s32[1,32]{1,0:T(1,128)}, u32[]{:S(2)}) copy-start(s32[1,32]{1,0:T(1,128)} %param.12) | copy-start | bytes 388
Sparse Core Ops, SparseCore 0:
  10.5 132.9 all-gather.4
  145.6 118.6 all-gather.6
where the time goes:
time: 345 us; the launch traced here: 343 us
  waiting for transfers between devices  122 us (35%)
  blocking collectives  96.5 us (28%)
  local copies, waits for them, and re-layouts  61.4 us (18%)
  matrix products  29.5 us (9%)
  other arithmetic  19.1 us (6%)
  between operations  13.5 us (4%)
    all_gather x1, waiting for transfers between devices, body(): value_piece = lax.all_gather(value_rows, 'tm', axis=0, tiled=True)  99.9 us
    all_gather x1, blocking collectives, body(): lax.all_gather(value_rows[None], 'stem', axis=0, tiled=True)  49.2 us
    all_gather x1, blocking collectives, body(): lax.all_gather(key_rows[None], 'stem', axis=0, tiled=True)  47.3 us
    all_gather x1, waiting for transfers between devices, body(): key_piece = lax.all_gather(key_rows, 'tm', axis=0, tiled=True)  21.6 us
    unnamed x12, local copies, waits for them, and re-layouts  20.6 us
    dot_general x8, matrix products, merge_block(): jnp.einsum('qhk,khd->qhd', weights.astype(jnp.bfloat16), value_block, pre...  11.7 us
    dot_general x8, matrix products, merge_block(): jnp.einsum('qhd,khd->qhk', queries, key_block, preferred_element_type=jnp...  11.2 us
    reshape x1, local copies, waits for them, and re-layouts, body(): value_piece.reshape(block_count, block_len, head_count, head_dim)  11.2 us
  transfers between devices with their start and end apart: 2, of which 2 were waited for; matrix products, arithmetic and copies ran while one was open for 10% of the time, Pallas kernels for 0%

commit v1 on v0

v1 whole, which is shorter than its diff:
```python
import functools
import math

import jax
import jax.numpy as jnp
from jax import lax
from jax.experimental import pallas as pl
from jax.experimental.pallas import tpu as pltpu
from jax.sharding import PartitionSpec as P

MESH = pl.DeviceIdType.MESH
F32 = jnp.float32
BF16 = jnp.bfloat16
LOG2E = math.log2(math.e)
NEG = -1e30
FR = 64
LANES = 128
QT = 256


def lane_iota(rows):
    return lax.broadcasted_iota(jnp.int32, (rows, LANES), 1)


def swap_halves(x):
    return pltpu.roll(x, 64, 1)


def nt_dot(a, b):
    return lax.dot_general(a, b, (((1,), (1,)), ((), ())), preferred_element_type=F32)


def unfold_queries(folded, z_ref, row):
    f = folded.astype(F32)
    low = lane_iota(32) < 64
    z_ref[pl.ds(row, 32), :] = jnp.where(low, f, 0.0).astype(BF16)
    z_ref[pl.ds(row + 32, 32), :] = jnp.where(low, swap_halves(f), 0.0).astype(BF16)


def ones_values(kv):
    return jnp.where(lane_iota(kv.shape[0]) < 64, jnp.ones_like(kv), kv)


def pack_part(m, acc):
    rows = acc.shape[0]
    lane = lane_iota(rows)
    total = jnp.where(lane < 64, acc, swap_halves(acc))
    value = acc / total
    lse = m + jnp.log(total)
    hi = lse.astype(BF16).astype(F32)
    mid = (lse - hi).astype(BF16).astype(F32)
    lo = lse - hi - mid
    return jnp.where(
        lane < 16, hi, jnp.where(lane < 32, mid, jnp.where(lane < 64, lo, value))
    ).astype(BF16)


def unpack_lse(part):
    return part[:, 0:1] + part[:, 16:17] + part[:, 32:33]


def kernel(
    hidden_ref, ids_ref, table_ref, act_ref, ada_ref, wqkv_hbm, wout_hbm, out_ref,
    wqkv, wout, resid, sb, kvb, qb, zb, rst, zst, mb, accb, biasb, selfm, ob, so, rt, rs,
    w_sem, zk_s, zk_r, zq_s, zq_r, st_s, st_r, y_s, y_r, f_s, c_s, c_r, tb_s, tb_r, sb_s, sb_r,
):
    s = lax.axis_index("stem")
    t = lax.axis_index("tm")
    z = lax.div(t, 8)
    y = lax.rem(lax.div(t, 2), 4)
    c = lax.rem(t, 2)
    y1 = y + 1 - 2 * lax.rem(y, 2)
    inner = jnp.logical_or(y == 1, y == 2)
    innerx = jnp.where(inner, 1, 0)
    p2 = jnp.where(inner, 3 - y, 3 - y1)
    p3 = jnp.where(inner, 3 - y1, 3 - y)
    peers = (y1, p2, p3)

    def at(zz, yy, cc):
        return (s, (zz * 4 + yy) * 2 + cc)

    def zpeer(d):
        return lax.rem(z + d, 8)

    def speer(d):
        return lax.rem(s + d, 8)

    core = at(z, y, 1 - c)

    barrier = pltpu.get_barrier_semaphore()
    for d in range(1, 8):
        pl.semaphore_signal(barrier, inc=1, device_id=at(zpeer(d), y, c), device_id_type=MESH)
        pl.semaphore_signal(barrier, inc=1, device_id=(speer(d), t), device_id_type=MESH)
    for p in peers:
        pl.semaphore_signal(barrier, inc=1, device_id=at(z, p, c), device_id_type=MESH)
    pl.semaphore_signal(barrier, inc=1, device_id=core, device_id_type=MESH)

    def wcopy(i):
        if i == 3:
            return pltpu.make_async_copy(wout_hbm, wout, w_sem.at[3])
        cols = pl.ds(i * 512, 512)
        return pltpu.make_async_copy(wqkv_hbm.at[:, cols], wqkv.at[i], w_sem.at[i])

    for i in (1, 2, 0, 3):
        wcopy(i).start()

    onehot = (lax.broadcasted_iota(jnp.int32, (128, FR), 0) == ids_ref[...]).astype(BF16)
    lookup = lax.dot_general(
        onehot, table_ref[...], (((0,), (0,)), ((), ())), preferred_element_type=F32
    )
    residual = hidden_ref[...].astype(F32) + lookup
    resid[...] = residual
    mean = jnp.mean(residual, axis=-1, keepdims=True)
    cent = residual - mean
    var = jnp.mean(jnp.square(cent), axis=-1, keepdims=True)
    normed = (cent * lax.rsqrt(var + 1e-6) * (1.0 + ada_ref[1:2, :]) + ada_ref[0:1, :]).astype(BF16)

    low = lane_iota(FR) < 64
    wcopy(1).wait()
    keys = jnp.dot(normed, wqkv[1], preferred_element_type=F32)
    wcopy(2).wait()
    values = jnp.dot(normed, wqkv[2], preferred_element_type=F32)
    for j in range(4):
        k2 = keys[:, 128 * j : 128 * j + 128]
        v2 = values[:, 128 * j : 128 * j + 128]
        sb[2 * j, 0:64, :] = jnp.where(low, k2, swap_halves(v2)).astype(BF16)
        sb[2 * j + 1, 0:64, :] = jnp.where(low, swap_halves(k2), v2).astype(BF16)

    pl.semaphore_wait(barrier, 18)

    def zk_copy(d):
        return pltpu.make_async_remote_copy(
            src_ref=sb.at[zpeer(d), pl.ds(0, 64)],
            dst_ref=kvb.at[y, c, pl.ds(pl.multiple_of(z * 64, 64), 64)],
            send_sem=zk_s.at[d], recv_sem=zk_r.at[d],
            device_id=at(zpeer(d), y, c), device_id_type=MESH,
        )

    def zq_copy(d):
        return pltpu.make_async_remote_copy(
            src_ref=sb.at[zpeer(d), pl.ds(64, 32)],
            dst_ref=qb.at[z],
            send_sem=zq_s.at[d], recv_sem=zq_r.at[d],
            device_id=at(zpeer(d), y, c), device_id_type=MESH,
        )

    def st_copy(d):
        return pltpu.make_async_remote_copy(
            src_ref=sb.at[speer(d)], dst_ref=rst.at[s],
            send_sem=st_s.at[d], recv_sem=st_r.at[d],
            device_id=(speer(d), t), device_id_type=MESH,
        )

    order = (4, 3, 5, 2, 6, 1, 7)
    for d in order:
        zk_copy(d).start()

    wcopy(0).wait()
    queries = jnp.dot(normed, wqkv[0], preferred_element_type=F32).astype(BF16).astype(F32) * 0.125
    low32 = lane_iota(32) < 64
    for j in range(4):
        q2 = queries[:, 128 * j : 128 * j + 128]
        a, b = q2[0:32], q2[32:64]
        sb[2 * j, 64:96, :] = jnp.where(low32, a, swap_halves(b)).astype(BF16)
        sb[2 * j + 1, 64:96, :] = jnp.where(low32, swap_halves(a), b).astype(BF16)
    for d in order:
        zq_copy(d).start()
    for d in order:
        st_copy(d).start()

    kvb[y, c, pl.ds(pl.multiple_of(z * 64, 64), 64), :] = sb[z, 0:64, :]
    qb[z] = sb[z, 64:96, :]
    rst[s] = sb[s]
    group = lax.div(lax.broadcasted_iota(jnp.int32, (8, 512), 1), 64)
    for yy in range(4):
        row = jnp.zeros((8, 512), F32)
        for zz in range(8):
            bias = jnp.where(act_ref[0, zz * 4 + yy] > 0, 0.0, NEG).astype(F32)
            row = jnp.where(group == zz, bias, row)
        biasb[yy] = row
    for j in range(4):
        q2 = queries[:, 128 * j : 128 * j + 128]
        k2 = keys[:, 128 * j : 128 * j + 128].astype(BF16).astype(F32)
        prod = q2 * k2
        even = jnp.sum(jnp.where(low, prod, 0.0), axis=1, keepdims=True)
        odd = jnp.sum(jnp.where(low, 0.0, prod), axis=1, keepdims=True)
        selfm[2 * j] = jnp.broadcast_to(even, (FR, LANES))
        selfm[2 * j + 1] = jnp.broadcast_to(odd, (FR, LANES))

    for d in order[::-1]:
        zk_copy(d).wait_recv()

    def c_copy(i, yy):
        return pltpu.make_async_remote_copy(
            src_ref=kvb.at[yy, c], dst_ref=kvb.at[yy, c],
            send_sem=c_s.at[i], recv_sem=c_r.at[i], device_id=core, device_id_type=MESH,
        )

    def c_arrival(i, yy):
        return pltpu.make_async_remote_copy(
            src_ref=kvb.at[yy, 1 - c], dst_ref=kvb.at[yy, 1 - c],
            send_sem=c_s.at[i], recv_sem=c_r.at[i], device_id=core, device_id_type=MESH,
        )

    def y_copy(block, target, ssem, rsem):
        return pltpu.make_async_remote_copy(
            src_ref=kvb.at[block, c], dst_ref=kvb.at[block, c],
            send_sem=ssem, recv_sem=rsem, device_id=at(z, target, c), device_id_type=MESH,
        )

    send_near = y_copy(y, y1, y_s.at[0], y_r.at[0])
    send_far = y_copy(y, p2, y_s.at[1], y_r.at[2 - innerx])
    send_far.start()
    send_near.start()
    c_copy(0, y).start()

    for d in order[::-1]:
        zq_copy(d).wait_recv()
    for zz in range(8):
        unfold_queries(qb[zz], zb, zz * 64)

    def step(kv_ref, bias, first):
        kv = kv_ref[...]
        w = ones_values(kv)

        @pl.loop(0, 512 // QT)
        def _(i):
            rows = pl.ds(pl.multiple_of(i * QT, QT), QT)
            sc = nt_dot(zb[rows, :], kv) + bias
            top = jnp.max(sc, axis=1, keepdims=True)
            if first:
                m = jnp.broadcast_to(top, (QT, LANES))
            else:
                old = mb[rows, :]
                m = jnp.maximum(old, top)
            p = jnp.exp2((sc - m[:, 0:1]) * LOG2E).astype(BF16)
            new = jnp.dot(p, w, preferred_element_type=F32)
            if first:
                accb[rows, :] = new
            else:
                accb[rows, :] = accb[rows, :] * jnp.exp2((old - m) * LOG2E) + new
            mb[rows, :] = m

    step(kvb.at[y, c], biasb[y, 0:1, :], True)
    c_arrival(0, y).wait_recv()
    step(kvb.at[y, 1 - c], biasb[y, 0:1, :], False)

    for d in order[::-1]:
        st_copy(d).wait_recv()
    for ss in range(8):
        unfold_queries(rst[ss, 64:96, :], zst, ss * 64)
    kvst = jnp.concatenate([rst[ss, 0:64, :] for ss in range(8)], axis=0)
    wst = ones_values(kvst)
    col = lax.broadcasted_iota(jnp.int32, (QT, 512), 1)

    @pl.loop(0, 512 // QT)
    def _(i):
        row0 = pl.multiple_of(i * QT, QT)
        rows = pl.ds(row0, QT)
        row = lax.broadcasted_iota(jnp.int32, (QT, 512), 0) + row0
        keep = jnp.logical_and(jnp.bitwise_and(row, 63) == jnp.bitwise_and(col, 63), row != col)
        sc = jnp.where(keep, nt_dot(zst[rows, :], kvst), NEG)
        top = jnp.max(sc, axis=1, keepdims=True)
        p = jnp.exp2((sc - top) * LOG2E).astype(BF16)
        so[rows, :] = pack_part(top, jnp.dot(p, wst, preferred_element_type=F32))

    def sb_copy(d):
        return pltpu.make_async_remote_copy(
            src_ref=so.at[pl.ds(pl.multiple_of(speer(d) * 64, 64), 64)], dst_ref=rs.at[s],
            send_sem=sb_s.at[d], recv_sem=sb_r.at[d],
            device_id=(speer(d), t), device_id_type=MESH,
        )

    for d in order:
        sb_copy(d).start()
    rs[s] = so[pl.ds(pl.multiple_of(s * 64, 64), 64), :]

    for i, p in enumerate(peers):
        y_copy(p, y1, y_s.at[0], y_r.at[i]).wait_recv()
        c_copy(i + 1, p).start()
        if i > 0:
            @pl.when(inner)
            def _():
                y_copy(p, y1, f_s.at[i], y_r.at[i]).start()
        step(kvb.at[p, c], biasb[p, 0:1, :], False)
        c_arrival(i + 1, p).wait_recv()
        step(kvb.at[p, 1 - c], biasb[p, 0:1, :], False)

    for zz in range(8):
        rows = slice(zz * 64, zz * 64 + 64)
        ob[zz] = pack_part(mb[rows, :], accb[rows, :])

    def tb_copy(d):
        return pltpu.make_async_remote_copy(
            src_ref=ob.at[zpeer(d)], dst_ref=rt.at[z],
            send_sem=tb_s.at[d], recv_sem=tb_r.at[d],
            device_id=at(zpeer(d), y, c), device_id_type=MESH,
        )

    for d in order:
        tb_copy(d).start()
    rt[z] = ob[z]

    for d in order[::-1]:
        sb_copy(d).wait_recv()
    for d in order[::-1]:
        tb_copy(d).wait_recv()

    own = act_ref[0, z * 4 + y] > 0
    halves = []
    for h in range(8):
        a = rs[h].astype(F32)
        b = rt[h].astype(F32)
        la = unpack_lse(a)
        lb = jnp.where(own, unpack_lse(b), selfm[h, :, 0:1])
        b = jnp.where(own, b, sb[h, 0:64, :].astype(F32))
        m = jnp.maximum(la, lb)
        wa = jnp.exp2((la - m) * LOG2E)
        wb = jnp.exp2((lb - m) * LOG2E)
        inv = 1.0 / (wa + wb)
        halves.append(a * (wa * inv) + b * (wb * inv))
    pairs = [
        jnp.where(low, swap_halves(halves[2 * j]), halves[2 * j + 1]).astype(BF16) for j in range(4)
    ]
    attended = jnp.concatenate(pairs, axis=1)
    wcopy(3).wait()
    branch = jnp.dot(attended, wout[...], preferred_element_type=F32)
    out_ref[...] = (resid[...] + ada_ref[2:3, :] * branch).astype(BF16)

    for d in order:
        zk_copy(d).wait_send()
        zq_copy(d).wait_send()
        st_copy(d).wait_send()
        sb_copy(d).wait_send()
        tb_copy(d).wait_send()
    send_near.wait_send()
    send_far.wait_send()
    for i, p in enumerate((y,) + peers):
        c_copy(i, p).wait_send()

    @pl.when(inner)
    def _():
        for i in (1, 2):
            y_copy(peers[i], y1, f_s.at[i], y_r.at[i]).wait_send()


def body(hidden, control_ids, control_table, activity, ada, w_qkv, w_out):
    vmem = pl.BlockSpec(memory_space=pltpu.VMEM)
    anywhere = pl.BlockSpec(memory_space=pl.ANY)
    dma = pltpu.SemaphoreType.DMA
    out = pl.pallas_call(
        kernel,
        name="attention_block",
        out_shape=jax.ShapeDtypeStruct((FR, 1024), BF16),
        in_specs=[vmem, vmem, vmem, pl.BlockSpec(memory_space=pltpu.SMEM), vmem, anywhere, anywhere],
        out_specs=vmem,
        scratch_shapes=[
            pltpu.VMEM((3, 1024, 512), BF16),
            pltpu.VMEM((512, 1024), BF16),
            pltpu.VMEM((FR, 1024), F32),
            pltpu.VMEM((8, 96, LANES), BF16),
            pltpu.VMEM((4, 2, 512, LANES), BF16),
            pltpu.VMEM((8, 32, LANES), BF16),
            pltpu.VMEM((512, LANES), BF16),
            pltpu.VMEM((8, 96, LANES), BF16),
            pltpu.VMEM((512, LANES), BF16),
            pltpu.VMEM((512, LANES), F32),
            pltpu.VMEM((512, LANES), F32),
            pltpu.VMEM((4, 8, 512), F32),
            pltpu.VMEM((8, FR, LANES), F32),
            pltpu.VMEM((8, FR, LANES), BF16),
            pltpu.VMEM((512, LANES), BF16),
            pltpu.VMEM((8, FR, LANES), BF16),
            pltpu.VMEM((8, FR, LANES), BF16),
            dma((4,)),
            dma((8,)), dma((8,)), dma((8,)), dma((8,)), dma((8,)), dma((8,)),
            dma((2,)), dma((3,)), dma((3,)), dma((4,)), dma((4,)),
            dma((8,)), dma((8,)), dma((8,)), dma((8,)),
        ],
        compiler_params=pltpu.CompilerParams(
            collective_id=0, has_side_effects=True, vmem_limit_bytes=40 * 1024 * 1024
        ),
    )(hidden[0], control_ids[None, :], control_table, activity, ada[0], w_qkv, w_out)
    return out[None]


def solution(mesh):
    placed = (P("stem", "tm", None), P("tm"), P(), P("stem", None), P("stem", None, None), P(), P())
    return jax.shard_map(
        body, mesh=mesh, in_specs=placed, out_specs=P("stem", "tm", None), check_vma=False
    )
```

time: 345 us -> 59 us (0.17)
  waiting for transfers between devices: 122 us -> 0 us
  blocking collectives: 96.5 us -> 0 us
  local copies, waits for them, and re-layouts: 61.4 us -> 7.64 us
  Pallas kernels: 0 us -> 51 us
  matrix products: 29.5 us -> 0 us
  other arithmetic: 19.1 us -> 0 us
  between operations: 13.5 us -> 0.02 us
    all_gather x2 -> x0, waiting for transfers between devices: 122 us -> none  [the longest x1 99.9 us: body(): value_piece = lax.all_gather(value_rows, 'tm', axis=0, tiled=True)]
    all_gather x2 -> x0, blocking collectives: 96.5 us -> none  [the longest x1 49.2 us: body(): lax.all_gather(value_rows[None], 'stem', axis=0, tiled=True)]
    pallas_call x0 -> x1, Pallas kernels: none -> 51 us  [body(): pl.pallas_call(kernel, name='attention_block', out_shape=jax.ShapeDtypeSt...]
    dot_general x20 -> x0, matrix products: 29.5 us -> none  [the longest x8 11.7 us: merge_block(): jnp.einsum('qhk,khd->qhd', weights.astype(jnp.bfloat16), value_block, pre...]
    reshape x6 -> x0, local copies, waits for them, and re-layouts: 28.7 us -> none  [the longest x1 11.2 us: body(): value_piece.reshape(block_count, block_len, head_count, head_dim)]
    unnamed x12 -> x14, local copies, waits for them, and re-layouts: 20.6 us -> 7.64 us
    dynamic_slice x8 -> x0, local copies, waits for them, and re-layouts: 10.2 us -> none  [body(): lax.scan(advance, running, (key_blocks, value_blocks, offsets))]
    reduce_sum x18 -> x0, other arithmetic: 9.12 us -> none  [the longest x9 6.06 us: bar_live(): return jnp.sum(jnp.where(hits, activity_row[None, :], 0), axis=1) > 0]
  transfers between devices with their start and end apart: 2 -> 0, of which waited for: 2 -> 0; matrix products, arithmetic and copies ran while one was open for 10% -> 0% of each run, Pallas kernels for 0% -> 0%
where the time goes in v1:
time: 59 us; the launch traced here: 58.7 us
  Pallas kernels  51 us (86%)
  local copies, waits for them, and re-layouts  7.64 us (13%)
    pallas_call x1, Pallas kernels, body(): pl.pallas_call(kernel, name='attention_block', out_shape=jax.ShapeDtypeSt...  51 us
    unnamed x14, local copies, waits for them, and re-layouts  7.64 us

profile of v1, /device:TPU:1, one launch (start us, length us, event | category | flops | bytes accessed | tf_op | source)
XLA Modules:
  0.0 58.7 jit_solution(7364373061437086079)
XLA Ops:
  0.0 0.7 %copy.10 = f32[1,3,1024]{2,1,0:T(4,128)S(1)} copy(f32[1,3,1024]{2,0,1:T(1,128)} %param.11) | data formatting | bytes 24576
  0.7 0.0 copy-start
  0.7 1.9 %copy-done = bf16[1024,1536]{1,0:T(8,128)(2,1)S(1)} copy-done((bf16[1024,1536]{1,0:T(8,128)(2,1)S(1)}, bf16[1024,1536]{1,0:T(8,128)(2,1)}, u32[]{:S(2)}) %copy-start) | copy-done | bytes 3145752
  2.6 0.0 copy-start.1
  2.6 1.2 %copy-done.1 = bf16[512,1024]{1,0:T(8,128)(2,1)S(1)} copy-done((bf16[512,1024]{1,0:T(8,128)(2,1)S(1)}, bf16[512,1024]{1,0:T(8,128)(2,1)}, u32[]{:S(2)}) %copy-start.1) | copy-done | bytes 1048600
  3.8 0.0 copy-start.2
  3.8 0.9 %copy-done.2 = bf16[128,1024]{1,0:T(8,128)(2,1)S(1)} copy-done((bf16[128,1024]{1,0:T(8,128)(2,1)S(1)}, bf16[128,1024]{1,0:T(8,128)(2,1)}, u32[]{:S(2)}) %copy-start.2) | copy-done | bytes 262168
  4.8 0.0 copy-start.3
  4.8 0.9 %copy-done.3 = bf16[1,64,1024]{2,1,0:T(8,128)(2,1)S(1)} copy-done((bf16[1,64,1024]{2,1,0:T(8,128)(2,1)S(1)}, bf16[1,64,1024]{2,1,0:T(8,128)(2,1)}, u32[]{:S(2)}) %copy-start.3) | copy-done | bytes 131096
  5.7 0.0 copy-start.4
  5.7 0.7 %copy-done.4 = s32[64]{0:T(128)S(1)} copy-done((s32[64]{0:T(128)S(1)}, s32[64]{0:T(128)}, u32[]{:S(2)}) %copy-start.4) | copy-done | bytes 280
  6.3 0.0 copy-start.5
  6.3 0.7 %copy-done.5 = s32[1,32]{1,0:T(1,128)S(1)} copy-done((s32[1,32]{1,0:T(1,128)S(1)}, s32[1,32]{1,0:T(1,128)}, u32[]{:S(2)}) %copy-start.5) | copy-done | bytes 152
  7.0 51.0 %attention_block.1 = bf16[64,1024]{1,0:T(8,128)(2,1)S(1)} custom-call(bf16[64,1024]{1,0:T(8,128)(2,1)S(1)} %bitcast.7, s32[1,64]{1,0:T(1,128)S(1)} %bitcast.9, bf16[128,1024]{1,0:T(8,128)(2,1)S(1)} %copy-done.2, s32[1,32]{1,0:T(1,128)S(1)} %copy-done.5, f32[3,1024]{1,0:T(4,128)S(1)} %bitcast.8, bf16[1024,1536]{1,0:T(8,128)(2,1)S(1)} %copy-done, ...), custom_call_target="tpu_custom_call" | custom-call | tf_op jit(solution)/shard_map/attention_block/pallas_call | solution.py:351
  58.0 0.7 %copy.12 = bf16[1,64,1024]{2,1,0:T(8,128)(2,1)} copy(bf16[1,64,1024]{2,1,0:T(8,128)(2,1)S(1)} %bitcast.6) | data formatting | bytes 262144
Async XLA Ops:
  0.7 1.9 %copy-start = (bf16[1024,1536]{1,0:T(8,128)(2,1)S(1)}, bf16[1024,1536]{1,0:T(8,128)(2,1)}, u32[]{:S(2)}) copy-start(bf16[1024,1536]{1,0:T(8,128)(2,1)} %wqkv_hbm.1) | copy-start | bytes 9437188
  2.6 1.2 %copy-start.1 = (bf16[512,1024]{1,0:T(8,128)(2,1)S(1)}, bf16[512,1024]{1,0:T(8,128)(2,1)}, u32[]{:S(2)}) copy-start(bf16[512,1024]{1,0:T(8,128)(2,1)} %wout_hbm.1) | copy-start | bytes 3145732
  3.8 0.9 %copy-start.2 = (bf16[128,1024]{1,0:T(8,128)(2,1)S(1)}, bf16[128,1024]{1,0:T(8,128)(2,1)}, u32[]{:S(2)}) copy-start(bf16[128,1024]{1,0:T(8,128)(2,1)} %table_ref.1) | copy-start | bytes 786436
  4.8 0.9 %copy-start.3 = (bf16[1,64,1024]{2,1,0:T(8,128)(2,1)S(1)}, bf16[1,64,1024]{2,1,0:T(8,128)(2,1)}, u32[]{:S(2)}) copy-start(bf16[1,64,1024]{2,1,0:T(8,128)(2,1)} %param.7) | copy-start | bytes 393220
  5.7 0.7 %copy-start.4 = (s32[64]{0:T(128)S(1)}, s32[64]{0:T(128)}, u32[]{:S(2)}) copy-start(s32[64]{0:T(128)} %param.8) | copy-start | bytes 772
  6.3 0.7 %copy-start.5 = (s32[1,32]{1,0:T(1,128)S(1)}, s32[1,32]{1,0:T(1,128)}, u32[]{:S(2)}) copy-start(s32[1,32]{1,0:T(1,128)} %act_ref.1) | copy-start | bytes 388

commit v2 on v1

v2 whole, which is shorter than its diff:
```python
import functools
import math

import jax
import jax.numpy as jnp
from jax import lax
from jax.experimental import pallas as pl
from jax.experimental.pallas import tpu as pltpu
from jax.sharding import PartitionSpec as P

MESH = pl.DeviceIdType.MESH
F32 = jnp.float32
BF16 = jnp.bfloat16
LOG2E = math.log2(math.e)
NEG = -1e30
FR = 64
LANES = 128
HALF = 256


def lane_iota(rows):
    return lax.broadcasted_iota(jnp.int32, (rows, LANES), 1)


def swap_halves(x):
    return pltpu.roll(x, 64, 1)


def nt_dot(a, b):
    return lax.dot_general(a, b, (((1,), (1,)), ((), ())), preferred_element_type=F32)


def unfold_low(f):
    return jnp.where(lane_iota(f.shape[0]) < 64, f, 0.0).astype(BF16)


def unfold_high(f):
    return unfold_low(swap_halves(f))


def ones_values(kv):
    return jnp.where(lane_iota(kv.shape[0]) < 64, jnp.ones_like(kv), kv)


def pack_part(m, acc):
    rows = acc.shape[0]
    lane = lane_iota(rows)
    total = jnp.where(lane < 64, acc, swap_halves(acc))
    value = acc / total
    lse = m + jnp.log(total)
    hi = lse.astype(BF16).astype(F32)
    mid = (lse - hi).astype(BF16).astype(F32)
    lo = lse - hi - mid
    return jnp.where(
        lane < 16, hi, jnp.where(lane < 32, mid, jnp.where(lane < 64, lo, value))
    ).astype(BF16)


def unpack_lse(part):
    return part[:, 0:1] + part[:, 16:17] + part[:, 32:33]


def kernel(
    hidden_ref, ids_ref, table_ref, act_ref, ada_ref, wqkv_hbm, wout_hbm, out_ref,
    wqkv, wout, resid, sb, kvb, qb, zb, rst, scb, mb, accb, biasb, selfm, ob, so, rt, rs,
    w_sem, zk_s, zk_r, zq_s, zq_r, st_s, st_r, y_s, y_r, f_s, c_s, c_r, tb_s, tb_r, sb_s, sb_r,
):
    s = lax.axis_index("stem")
    t = lax.axis_index("tm")
    z = lax.div(t, 8)
    y = lax.rem(lax.div(t, 2), 4)
    c = lax.rem(t, 2)
    y1 = y + 1 - 2 * lax.rem(y, 2)
    inner = jnp.logical_or(y == 1, y == 2)
    innerx = jnp.where(inner, 1, 0)
    p2 = jnp.where(inner, 3 - y, 3 - y1)
    p3 = jnp.where(inner, 3 - y1, 3 - y)
    peers = (y1, p2, p3)

    def at(zz, yy, cc):
        return (s, (zz * 4 + yy) * 2 + cc)

    def zpeer(d):
        return lax.rem(z + d, 8)

    def speer(d):
        return lax.rem(s + d, 8)

    core = at(z, y, 1 - c)

    barrier = pltpu.get_barrier_semaphore()
    for d in range(1, 8):
        pl.semaphore_signal(barrier, inc=1, device_id=at(zpeer(d), y, c), device_id_type=MESH)
        pl.semaphore_signal(barrier, inc=1, device_id=(speer(d), t), device_id_type=MESH)
    for p in peers:
        pl.semaphore_signal(barrier, inc=1, device_id=at(z, p, c), device_id_type=MESH)
    pl.semaphore_signal(barrier, inc=1, device_id=core, device_id_type=MESH)

    def wcopy(i):
        if i == 3:
            return pltpu.make_async_copy(wout_hbm, wout, w_sem.at[3])
        cols = pl.ds(i * 512, 512)
        return pltpu.make_async_copy(wqkv_hbm.at[:, cols], wqkv.at[i], w_sem.at[i])

    for i in (1, 2, 0, 3):
        wcopy(i).start()

    def ada_row(i):
        return jnp.concatenate([ada_ref[8 * i + k : 8 * i + k + 1, :] for k in range(8)], axis=1)

    onehot = (lax.broadcasted_iota(jnp.int32, (128, FR), 0) == ids_ref[...]).astype(BF16)
    lookup = lax.dot_general(
        onehot, table_ref[...], (((0,), (0,)), ((), ())), preferred_element_type=F32
    )
    residual = hidden_ref[...].astype(F32) + lookup
    resid[...] = residual
    mean = jnp.mean(residual, axis=-1, keepdims=True)
    cent = residual - mean
    var = jnp.mean(jnp.square(cent), axis=-1, keepdims=True)
    normed = (cent * lax.rsqrt(var + 1e-6) * (1.0 + ada_row(1)) + ada_row(0)).astype(BF16)

    low = lane_iota(FR) < 64
    wcopy(1).wait()
    keys = jnp.dot(normed, wqkv[1], preferred_element_type=F32)
    wcopy(2).wait()
    values = jnp.dot(normed, wqkv[2], preferred_element_type=F32)
    for j in range(4):
        k2 = keys[:, 128 * j : 128 * j + 128]
        v2 = values[:, 128 * j : 128 * j + 128]
        sb[2 * j, 0:64, :] = jnp.where(low, k2, swap_halves(v2)).astype(BF16)
        sb[2 * j + 1, 0:64, :] = jnp.where(low, swap_halves(k2), v2).astype(BF16)

    pl.semaphore_wait(barrier, 18)

    def zk_copy(d):
        return pltpu.make_async_remote_copy(
            src_ref=sb.at[zpeer(d), pl.ds(0, 64)],
            dst_ref=kvb.at[y, c, pl.ds(pl.multiple_of(z * 64, 64), 64)],
            send_sem=zk_s.at[d], recv_sem=zk_r.at[z],
            device_id=at(zpeer(d), y, c), device_id_type=MESH,
        )

    def zq_copy(d):
        return pltpu.make_async_remote_copy(
            src_ref=sb.at[zpeer(d), pl.ds(64, 32)],
            dst_ref=qb.at[z],
            send_sem=zq_s.at[d], recv_sem=zq_r.at[z],
            device_id=at(zpeer(d), y, c), device_id_type=MESH,
        )

    def st_copy(d):
        return pltpu.make_async_remote_copy(
            src_ref=sb.at[speer(d)], dst_ref=rst.at[s],
            send_sem=st_s.at[d], recv_sem=st_r.at[d],
            device_id=(speer(d), t), device_id_type=MESH,
        )

    order = (4, 3, 5, 2, 6, 1, 7)
    for d in order:
        zk_copy(d).start()

    wcopy(0).wait()
    queries = jnp.dot(normed, wqkv[0], preferred_element_type=F32).astype(BF16).astype(F32) * 0.125
    low32 = lane_iota(32) < 64
    for j in range(4):
        q2 = queries[:, 128 * j : 128 * j + 128]
        a, b = q2[0:32], q2[32:64]
        sb[2 * j, 64:96, :] = jnp.where(low32, a, swap_halves(b)).astype(BF16)
        sb[2 * j + 1, 64:96, :] = jnp.where(low32, swap_halves(a), b).astype(BF16)
    for d in order:
        zq_copy(d).start()
    for d in order:
        st_copy(d).start()

    own_kv = pltpu.make_async_copy(
        sb.at[z, pl.ds(0, 64)], kvb.at[y, c, pl.ds(pl.multiple_of(z * 64, 64), 64)], zk_r.at[z]
    )
    own_kv.start()
    own_q = pltpu.make_async_copy(sb.at[z, pl.ds(64, 32)], qb.at[z], zq_r.at[z])
    own_q.start()
    rst[s] = sb[s]
    group = lax.div(lax.broadcasted_iota(jnp.int32, (8, 512), 1), 64)
    for yy in range(4):
        row = jnp.zeros((8, 512), F32)
        for zz in range(8):
            bias = jnp.where(act_ref[0, zz * 4 + yy] > 0, 0.0, NEG).astype(F32)
            row = jnp.where(group == zz, bias, row)
        biasb[yy] = row
    for j in range(4):
        q2 = queries[:, 128 * j : 128 * j + 128]
        k2 = keys[:, 128 * j : 128 * j + 128].astype(BF16).astype(F32)
        prod = q2 * k2
        even = jnp.sum(jnp.where(low, prod, 0.0), axis=1, keepdims=True)
        odd = jnp.sum(jnp.where(low, 0.0, prod), axis=1, keepdims=True)
        selfm[2 * j] = jnp.broadcast_to(even, (FR, LANES))
        selfm[2 * j + 1] = jnp.broadcast_to(odd, (FR, LANES))

    def zk_wait(zz):
        block = kvb.at[y, c, pl.ds(zz * 64, 64)]
        pltpu.make_async_copy(block, block, zk_r.at[zz]).wait()

    def zq_wait(zz):
        pltpu.make_async_copy(qb.at[zz], qb.at[zz], zq_r.at[zz]).wait()

    def part(yy, cc, g):
        return kvb.at[yy, cc, pl.ds(g * HALF, HALF)]

    def c_copy(i, yy, g):
        return pltpu.make_async_remote_copy(
            src_ref=part(yy, c, g), dst_ref=part(yy, c, g),
            send_sem=c_s.at[4 * g + i], recv_sem=c_r.at[4 * g + i], device_id=core, device_id_type=MESH,
        )

    def c_arrival(i, yy, g):
        return pltpu.make_async_remote_copy(
            src_ref=part(yy, 1 - c, g), dst_ref=part(yy, 1 - c, g),
            send_sem=c_s.at[4 * g + i], recv_sem=c_r.at[4 * g + i], device_id=core, device_id_type=MESH,
        )

    def y_copy(block, target, ssem, rsem, g):
        return pltpu.make_async_remote_copy(
            src_ref=part(block, c, g), dst_ref=part(block, c, g),
            send_sem=ssem, recv_sem=rsem, device_id=at(z, target, c), device_id_type=MESH,
        )

    def send_near(g):
        return y_copy(y, y1, y_s.at[2 * g], y_r.at[3 * g], g)

    def send_far(g):
        return y_copy(y, p2, y_s.at[2 * g + 1], y_r.at[3 * g + 2 - innerx], g)

    def onward(i, g):
        return y_copy(peers[i], y1, f_s.at[2 * g + i - 1], y_r.at[3 * g + i], g)

    def gather_z(g):
        for zz in range(4 * g, 4 * g + 4):
            zk_wait(zz)
        send_far(g).start()
        send_near(g).start()
        c_copy(0, y, g).start()

    def gather_y(g):
        for i, p in enumerate(peers):
            y_copy(p, y1, y_s.at[2 * g], y_r.at[3 * g + i], g).wait_recv()
            if i > 0:
                @pl.when(inner)
                def _():
                    onward(i, g).start()
            c_copy(i + 1, p, g).start()

    def gather_core(g):
        for i, p in enumerate((y,) + peers):
            c_arrival(i, p, g).wait_recv()

    def take_queries(g):
        for zz in range(4 * g, 4 * g + 4):
            zq_wait(zz)
            f = qb[zz].astype(F32)
            zb[zz * 64 : zz * 64 + 32, :] = unfold_low(f)
            zb[zz * 64 + 32 : zz * 64 + 64, :] = unfold_high(f)

    def cell(g, kg):
        rows = slice(g * HALF, g * HALF + HALF)
        keys_at = [(yy, cc) for yy in range(4) for cc in range(2)]
        zq = zb[rows, :]
        top = None
        for b, (yy, cc) in enumerate(keys_at):
            kv = kvb[yy, cc, kg * HALF : kg * HALF + HALF, :]
            sc = nt_dot(zq, kv) + biasb[yy, 0:1, kg * HALF : kg * HALF + HALF]
            scb[kg, :, b * HALF : b * HALF + HALF] = sc
            for k in range(0, HALF, LANES):
                one = sc[:, k : k + LANES]
                top = one if top is None else jnp.maximum(top, one)
        m = jnp.broadcast_to(jnp.max(top, axis=1, keepdims=True), (HALF, LANES))
        if kg > 0:
            old = mb[rows, :]
            m = jnp.maximum(old, m)
        total = None
        for b, (yy, cc) in enumerate(keys_at):
            kv = kvb[yy, cc, kg * HALF : kg * HALF + HALF, :]
            p = jnp.exp2((scb[kg, :, b * HALF : b * HALF + HALF] - m[:, 0:1]) * LOG2E).astype(BF16)
            new = jnp.dot(p, ones_values(kv), preferred_element_type=F32)
            total = new if total is None else total + new
        if kg > 0:
            total = accb[rows, :] * jnp.exp2((old - m) * LOG2E) + total
        else:
            accb[rows, :] = total
            mb[rows, :] = m
        return m, total

    def tb_copy(zz):
        return pltpu.make_async_remote_copy(
            src_ref=ob.at[zz], dst_ref=rt.at[z],
            send_sem=tb_s.at[zz], recv_sem=tb_r.at[z],
            device_id=at(zz, y, c), device_id_type=MESH,
        )

    def give_back(g, m, total):
        packed = pack_part(m, total)
        for k in range(4):
            zz = 4 * g + k
            ob[zz] = packed[64 * k : 64 * k + 64, :]

            @pl.when(z != zz)
            def _():
                tb_copy(zz).start()

            @pl.when(z == zz)
            def _():
                pltpu.make_async_copy(ob.at[zz], rt.at[zz], tb_r.at[zz]).start()

    gather_z(0)
    take_queries(0)
    gather_z(1)
    gather_y(0)
    take_queries(1)
    gather_core(0)
    cell(0, 0)
    gather_y(1)

    for d in order[::-1]:
        st_copy(d).wait_recv()
    row = lax.broadcasted_iota(jnp.int32, (LANES, LANES), 0)
    col = lax.broadcasted_iota(jnp.int32, (LANES, LANES), 1)
    keep = jnp.logical_and(jnp.bitwise_and(row, 15) == jnp.bitwise_and(col, 15), row != col)
    for f0 in range(0, FR, 16):
        q0 = 64 + f0 % 32
        folded = jnp.concatenate([rst[ss, q0 : q0 + 16, :] for ss in range(8)], axis=0).astype(F32)
        qst = unfold_low(folded) if f0 < 32 else unfold_high(folded)
        kvst = jnp.concatenate([rst[ss, f0 : f0 + 16, :] for ss in range(8)], axis=0)
        sc = jnp.where(keep, nt_dot(qst, kvst), NEG)
        top = jnp.max(sc, axis=1, keepdims=True)
        p = jnp.exp2((sc - top) * LOG2E).astype(BF16)
        done = pack_part(top, jnp.dot(p, ones_values(kvst), preferred_element_type=F32))
        for ss in range(8):
            so[ss, f0 : f0 + 16, :] = done[16 * ss : 16 * ss + 16, :]

    def sb_copy(d):
        return pltpu.make_async_remote_copy(
            src_ref=so.at[speer(d)], dst_ref=rs.at[s],
            send_sem=sb_s.at[d], recv_sem=sb_r.at[d],
            device_id=(speer(d), t), device_id_type=MESH,
        )

    for d in order:
        sb_copy(d).start()
    rs[s] = so[s]

    gather_core(1)
    give_back(0, *cell(0, 1))
    cell(1, 0)
    give_back(1, *cell(1, 1))

    for d in order[::-1]:
        sb_copy(d).wait_recv()
    for zz in range(8):
        pltpu.make_async_copy(rt.at[zz], rt.at[zz], tb_r.at[zz]).wait()

    own = act_ref[0, z * 4 + y] > 0
    halves = []
    for h in range(8):
        a = rs[h].astype(F32)
        b = rt[h].astype(F32)
        la = unpack_lse(a)
        lb = jnp.where(own, unpack_lse(b), selfm[h, :, 0:1])
        b = jnp.where(own, b, sb[h, 0:64, :].astype(F32))
        m = jnp.maximum(la, lb)
        wa = jnp.exp2((la - m) * LOG2E)
        wb = jnp.exp2((lb - m) * LOG2E)
        inv = 1.0 / (wa + wb)
        halves.append(a * (wa * inv) + b * (wb * inv))
    pairs = [
        jnp.where(low, swap_halves(halves[2 * j]), halves[2 * j + 1]).astype(BF16) for j in range(4)
    ]
    attended = jnp.concatenate(pairs, axis=1)
    wcopy(3).wait()
    branch = jnp.dot(attended, wout[...], preferred_element_type=F32)
    out_ref[...] = (resid[...] + ada_row(2) * branch).astype(BF16)

    for d in order:
        zk_copy(d).wait_send()
        zq_copy(d).wait_send()
        st_copy(d).wait_send()
        sb_copy(d).wait_send()
    for zz in range(8):
        @pl.when(z != zz)
        def _():
            tb_copy(zz).wait_send()
    for g in range(2):
        send_near(g).wait_send()
        send_far(g).wait_send()
        for i, p in enumerate((y,) + peers):
            c_copy(i, p, g).wait_send()

        @pl.when(inner)
        def _():
            for i in (1, 2):
                onward(i, g).wait_send()


def body(hidden, control_ids, control_table, activity, ada, w_qkv, w_out):
    vmem = pl.BlockSpec(memory_space=pltpu.VMEM)
    anywhere = pl.BlockSpec(memory_space=pl.ANY)
    dma = pltpu.SemaphoreType.DMA
    out = pl.pallas_call(
        kernel,
        name="attention_block",
        out_shape=jax.ShapeDtypeStruct((FR, 1024), BF16),
        in_specs=[vmem, vmem, vmem, pl.BlockSpec(memory_space=pltpu.SMEM), vmem, anywhere, anywhere],
        out_specs=vmem,
        scratch_shapes=[
            pltpu.VMEM((3, 1024, 512), BF16),
            pltpu.VMEM((512, 1024), BF16),
            pltpu.VMEM((FR, 1024), F32),
            pltpu.VMEM((8, 96, LANES), BF16),
            pltpu.VMEM((4, 2, 512, LANES), BF16),
            pltpu.VMEM((8, 32, LANES), BF16),
            pltpu.VMEM((512, LANES), BF16),
            pltpu.VMEM((8, 96, LANES), BF16),
            pltpu.VMEM((2, HALF, 8 * HALF), F32),
            pltpu.VMEM((512, LANES), F32),
            pltpu.VMEM((512, LANES), F32),
            pltpu.VMEM((4, 8, 512), F32),
            pltpu.VMEM((8, FR, LANES), F32),
            pltpu.VMEM((8, FR, LANES), BF16),
            pltpu.VMEM((8, FR, LANES), BF16),
            pltpu.VMEM((8, FR, LANES), BF16),
            pltpu.VMEM((8, FR, LANES), BF16),
            dma((4,)),
            dma((8,)), dma((8,)), dma((8,)), dma((8,)), dma((8,)), dma((8,)),
            dma((4,)), dma((6,)), dma((4,)), dma((8,)), dma((8,)),
            dma((8,)), dma((8,)), dma((8,)), dma((8,)),
        ],
        compiler_params=pltpu.CompilerParams(
            collective_id=0, has_side_effects=True, vmem_limit_bytes=60 * 1024 * 1024
        ),
    )(hidden[0], control_ids[None, :], control_table, activity, ada.reshape(24, LANES), w_qkv, w_out)
    return out[None]


def solution(mesh):
    placed = (P("stem", "tm", None), P("tm"), P(), P("stem", None), P("stem", None, None), P(), P())
    return jax.shard_map(
        body, mesh=mesh, in_specs=placed, out_specs=P("stem", "tm", None), check_vma=False
    )
```

time: 59 us -> 46.9 us (0.79)
  local copies, waits for them, and re-layouts: 7.64 us -> 1.57 us
  Pallas kernels: 51 us -> 45.2 us
    unnamed x14 -> x1, local copies, waits for them, and re-layouts: 7.64 us -> 1.57 us
    pallas_call x1, Pallas kernels: 51 us -> 45.2 us  [body(): pl.pallas_call(kernel, name='attention_block', out_shape=jax.ShapeDtypeSt...]
where the time goes in v2:
time: 46.9 us; the launch traced here: 46.7 us
  Pallas kernels  45.2 us (96%)
  local copies, waits for them, and re-layouts  1.57 us (3%)
    pallas_call x1, Pallas kernels, body(): pl.pallas_call(kernel, name='attention_block', out_shape=jax.ShapeDtypeSt...  45.2 us
    unnamed x1, local copies, waits for them, and re-layouts  1.57 us

profile of v2, /device:TPU:1, one launch (start us, length us, event | category | flops | bytes accessed | tf_op | source)
XLA Modules:
  0.0 46.7 jit_solution(5890847417802441917)
XLA Ops:
  0.0 45.2 %attention_block.1 = bf16[64,1024]{1,0:T(8,128)(2,1)} custom-call(bf16[64,1024]{1,0:T(8,128)(2,1)} %bitcast.5, s32[1,64]{1,0:T(1,128)} %bitcast.7, bf16[128,1024]{1,0:T(8,128)(2,1)} %table_ref.1, s32[1,32]{1,0:T(1,128)} %act_ref.1, f32[24,128]{1,0:T(8,128)} %bitcast.6, bf16[1024,1536]{1,0:T(8,128)(2,1)} %wqkv_hbm.1, bf16[512,1024]{1,0:T(8,128)(2,1)} %wout_hbm.1), custom_call_target="tpu_custom_call" | custom-call | tf_op jit(solution)/shard_map/attention_block/pallas_call | solution.py:405
  45.2 1.6 %copy.9 = bf16[1,64,1024]{2,1,0:T(8,128)(2,1)} copy(bf16[1,64,1024]{2,1,0:T(8,128)(2,1)} %bitcast.4) | data formatting | bytes 262144

commit v3 on v2

--- a/solution.py
+++ b/solution.py
@@ -61,9 +61,10 @@
 
 
 def kernel(
-    hidden_ref, ids_ref, table_ref, act_ref, ada_ref, wqkv_hbm, wout_hbm, out_ref,
-    wqkv, wout, resid, sb, kvb, qb, zb, rst, scb, mb, accb, biasb, selfm, ob, so, rt, rs,
-    w_sem, zk_s, zk_r, zq_s, zq_r, st_s, st_r, y_s, y_r, f_s, c_s, c_r, tb_s, tb_r, sb_s, sb_r,
+    hidden_hbm, ids_hbm, table_hbm, act_hbm, ada_hbm, wqkv_hbm, wout_hbm, out_ref,
+    hidden_ref, ids_ref, table_ref, act_ref, ada_ref,
+    wqkv, wout, resid, sb, kvb, qb, qo, zb, zo, rst, scb, mb, accb, biasb, selfm, ob, oo, so, rt, ro, rs,
+    i_sem, w_sem, zk_s, zk_r, zq_s, zq_r, st_s, st_r, y_s, y_r, f_s, c_s, c_r, o_s, o_r, u_s, u_r, tb_s, tb_r, sb_s, sb_r,
 ):
     s = lax.axis_index("stem")
     t = lax.axis_index("tm")
@@ -72,10 +73,9 @@
     c = lax.rem(t, 2)
     y1 = y + 1 - 2 * lax.rem(y, 2)
     inner = jnp.logical_or(y == 1, y == 2)
-    innerx = jnp.where(inner, 1, 0)
-    p2 = jnp.where(inner, 3 - y, 3 - y1)
-    p3 = jnp.where(inner, 3 - y1, 3 - y)
-    peers = (y1, p2, p3)
+    outer = jnp.logical_not(inner)
+    far_inner = 3 - y
+    pair = lax.div(y, 2)
 
     def at(zz, yy, cc):
         return (s, (zz * 4 + yy) * 2 + cc)
@@ -92,8 +92,17 @@
     for d in range(1, 8):
         pl.semaphore_signal(barrier, inc=1, device_id=at(zpeer(d), y, c), device_id_type=MESH)
         pl.semaphore_signal(barrier, inc=1, device_id=(speer(d), t), device_id_type=MESH)
-    for p in peers:
-        pl.semaphore_signal(barrier, inc=1, device_id=at(z, p, c), device_id_type=MESH)
+    pl.semaphore_signal(barrier, inc=1, device_id=at(z, y1, c), device_id_type=MESH)
+
+    @pl.when(inner)
+    def _():
+        pl.semaphore_signal(barrier, inc=1, device_id=at(z, far_inner, c), device_id_type=MESH)
+
+    @pl.when(outer)
+    def _():
+        for d in range(1, 8):
+            pl.semaphore_signal(barrier, inc=1, device_id=at(zpeer(d), y1, c), device_id_type=MESH)
+
     pl.semaphore_signal(barrier, inc=1, device_id=core, device_id_type=MESH)
 
     def wcopy(i):
@@ -102,8 +111,21 @@
         cols = pl.ds(i * 512, 512)
         return pltpu.make_async_copy(wqkv_hbm.at[:, cols], wqkv.at[i], w_sem.at[i])
 
+    small = [
+        pltpu.make_async_copy(src, dst, i_sem.at[n])
+        for n, (src, dst) in enumerate(
+            (
+                (hidden_hbm, hidden_ref), (ids_hbm, ids_ref), (table_hbm, table_ref),
+                (ada_hbm, ada_ref), (act_hbm, act_ref),
+            )
+        )
+    ]
+    for copy in small:
+        copy.start()
     for i in (1, 2, 0, 3):
         wcopy(i).start()
+    for copy in small:
+        copy.wait()
 
     def ada_row(i):
         return jnp.concatenate([ada_ref[8 * i + k : 8 * i + k + 1, :] for k in range(8)], axis=1)
@@ -130,7 +152,7 @@
         sb[2 * j, 0:64, :] = jnp.where(low, k2, swap_halves(v2)).astype(BF16)
         sb[2 * j + 1, 0:64, :] = jnp.where(low, swap_halves(k2), v2).astype(BF16)
 
-    pl.semaphore_wait(barrier, 18)
+    pl.semaphore_wait(barrier, jnp.where(inner, 24, 16))
 
     def zk_copy(d):
         return pltpu.make_async_remote_copy(
@@ -205,15 +227,17 @@
     def part(yy, cc, g):
         return kvb.at[yy, cc, pl.ds(g * HALF, HALF)]
 
-    def c_copy(i, yy, g):
-        return pltpu.make_async_remote_copy(
-            src_ref=part(yy, c, g), dst_ref=part(yy, c, g),
+    held = (y, y1, far_inner, jnp.where(inner, 3 - y1, 0))
+
+    def c_copy(i, g):
+        return pltpu.make_async_remote_copy(
+            src_ref=part(held[i], c, g), dst_ref=part(held[i], c, g),
             send_sem=c_s.at[4 * g + i], recv_sem=c_r.at[4 * g + i], device_id=core, device_id_type=MESH,
         )
 
-    def c_arrival(i, yy, g):
-        return pltpu.make_async_remote_copy(
-            src_ref=part(yy, 1 - c, g), dst_ref=part(yy, 1 - c, g),
+    def c_arrival(i, g):
+        return pltpu.make_async_remote_copy(
+            src_ref=part(held[i], 1 - c, g), dst_ref=part(held[i], 1 - c, g),
             send_sem=c_s.at[4 * g + i], recv_sem=c_r.at[4 * g + i], device_id=core, device_id_type=MESH,
         )
 
@@ -227,66 +251,77 @@
         return y_copy(y, y1, y_s.at[2 * g], y_r.at[3 * g], g)
 
     def send_far(g):
-        return y_copy(y, p2, y_s.at[2 * g + 1], y_r.at[3 * g + 2 - innerx], g)
-
-    def onward(i, g):
-        return y_copy(peers[i], y1, f_s.at[2 * g + i - 1], y_r.at[3 * g + i], g)
+        return y_copy(y, far_inner, y_s.at[2 * g + 1], y_r.at[3 * g + 1], g)
+
+    def onward(g):
+        return y_copy(y1, far_inner, f_s.at[g], y_r.at[3 * g + 2], g)
+
+    def lend_queries():
+        return pltpu.make_async_remote_copy(
+            src_ref=qb, dst_ref=qo, send_sem=o_s, recv_sem=o_r,
+            device_id=at(z, y1, c), device_id_type=MESH,
+        )
 
     def gather_z(g):
         for zz in range(4 * g, 4 * g + 4):
             zk_wait(zz)
-        send_far(g).start()
+
+        @pl.when(inner)
+        def _():
+            send_far(g).start()
+
         send_near(g).start()
-        c_copy(0, y, g).start()
-
-    def gather_y(g):
-        for i, p in enumerate(peers):
-            y_copy(p, y1, y_s.at[2 * g], y_r.at[3 * g + i], g).wait_recv()
-            if i > 0:
-                @pl.when(inner)
-                def _():
-                    onward(i, g).start()
-            c_copy(i + 1, p, g).start()
-
-    def gather_core(g):
-        for i, p in enumerate((y,) + peers):
-            c_arrival(i, p, g).wait_recv()
-
-    def take_queries(g):
-        for zz in range(4 * g, 4 * g + 4):
-            zq_wait(zz)
-            f = qb[zz].astype(F32)
-            zb[zz * 64 : zz * 64 + 32, :] = unfold_low(f)
-            zb[zz * 64 + 32 : zz * 64 + 64, :] = unfold_high(f)
-
-    def cell(g, kg):
+        c_copy(0, g).start()
+
+    def gather_near(g):
+        y_copy(y1, y1, y_s.at[2 * g], y_r.at[3 * g], g).wait_recv()
+
+        @pl.when(inner)
+        def _():
+            onward(g).start()
+
+        c_copy(1, g).start()
+
+    def gather_far(i, g):
+        y_copy(held[i], far_inner, f_s.at[g], y_r.at[3 * g + i - 1], g).wait_recv()
+        c_copy(i, g).start()
+
+    def gather_core(i):
+        for g in range(2):
+            c_arrival(i, g).wait_recv()
+
+    def unfold(source, target):
+        for zz in range(8):
+            f = source[zz].astype(F32)
+            target[zz * 64 : zz * 64 + 32, :] = unfold_low(f)
+            target[zz * 64 + 32 : zz * 64 + 64, :] = unfold_high(f)
+
+    def cell(queries_ref, g, which, old=None):
         rows = slice(g * HALF, g * HALF + HALF)
-        keys_at = [(yy, cc) for yy in range(4) for cc in range(2)]
-        zq = zb[rows, :]
+        keys_at = [(2 * which + i, cc) for i in range(2) for cc in range(2)]
+        zq = queries_ref[rows, :]
         top = None
         for b, (yy, cc) in enumerate(keys_at):
-            kv = kvb[yy, cc, kg * HALF : kg * HALF + HALF, :]
-            sc = nt_dot(zq, kv) + biasb[yy, 0:1, kg * HALF : kg * HALF + HALF]
-            scb[kg, :, b * HALF : b * HALF + HALF] = sc
-            for k in range(0, HALF, LANES):
+            sc = nt_dot(zq, kvb[yy, cc]) + biasb[yy, 0:1, :]
+            scb[g, :, 512 * b : 512 * b + 512] = sc
+            for k in range(0, 512, LANES):
                 one = sc[:, k : k + LANES]
                 top = one if top is None else jnp.maximum(top, one)
         m = jnp.broadcast_to(jnp.max(top, axis=1, keepdims=True), (HALF, LANES))
-        if kg > 0:
-            old = mb[rows, :]
-            m = jnp.maximum(old, m)
+        if old is not None:
+            m = jnp.maximum(old[0], m)
         total = None
         for b, (yy, cc) in enumerate(keys_at):
-            kv = kvb[yy, cc, kg * HALF : kg * HALF + HALF, :]
-            p = jnp.exp2((scb[kg, :, b * HALF : b * HALF + HALF] - m[:, 0:1]) * LOG2E).astype(BF16)
-            new = jnp.dot(p, ones_values(kv), preferred_element_type=F32)
+            p = jnp.exp2((scb[g, :, 512 * b : 512 * b + 512] - m[:, 0:1]) * LOG2E).astype(BF16)
+            new = jnp.dot(p, ones_values(kvb[yy, cc]), preferred_element_type=F32)
             total = new if total is None else total + new
-        if kg > 0:
-            total = accb[rows, :] * jnp.exp2((old - m) * LOG2E) + total
-        else:
-            accb[rows, :] = total
-            mb[rows, :] = m
+        if old is not None:
+            total = old[1] * jnp.exp2((old[0] - m) * LOG2E) + total
         return m, total
+
+    def kept(g):
+        rows = slice(g * HALF, g * HALF + HALF)
+        return mb[rows, :], accb[rows, :]
 
     def tb_copy(zz):
         return pltpu.make_async_remote_copy(
@@ -294,6 +329,20 @@
             send_sem=tb_s.at[zz], recv_sem=tb_r.at[z],
             device_id=at(zz, y, c), device_id_type=MESH,
         )
+
+    def tu_copy(zz):
+        return pltpu.make_async_remote_copy(
+            src_ref=oo.at[zz], dst_ref=ro.at[z],
+            send_sem=u_s.at[zz], recv_sem=u_r.at[z],
+            device_id=at(zz, y1, c), device_id_type=MESH,
+        )
+
+    def give_lent(g, m, total):
+        packed = pack_part(m, total)
+        for k in range(4):
+            zz = 4 * g + k
+            oo[zz] = packed[64 * k : 64 * k + 64, :]
+            tu_copy(zz).start()
 
     def give_back(g, m, total):
         packed = pack_part(m, total)
@@ -310,13 +359,41 @@
                 pltpu.make_async_copy(ob.at[zz], rt.at[zz], tb_r.at[zz]).start()
 
     gather_z(0)
-    take_queries(0)
     gather_z(1)
-    gather_y(0)
-    take_queries(1)
+    for zz in range(8):
+        zq_wait(zz)
+
+    @pl.when(outer)
+    def _():
+        lend_queries().start()
+
+    unfold(qb, zb)
+    for g in range(2):
+        gather_near(g)
+
+    @pl.when(inner)
+    def _():
+        for g in range(2):
+            gather_far(2, g)
+        lend_queries().wait_recv()
+        unfold(qo, zo)
+
     gather_core(0)
-    cell(0, 0)
-    gather_y(1)
+    gather_core(1)
+    for g in range(2):
+        m, total = cell(zb, g, pair)
+        mb[g * HALF : g * HALF + HALF, :] = m
+        accb[g * HALF : g * HALF + HALF, :] = total
+
+    @pl.when(outer)
+    def _():
+        for g in range(2):
+            give_back(g, *kept(g))
+
+    @pl.when(inner)
+    def _():
+        for g in range(2):
+            gather_far(3, g)
 
     for d in order[::-1]:
         st_copy(d).wait_recv()
@@ -346,15 +423,28 @@
         sb_copy(d).start()
     rs[s] = so[s]
 
-    gather_core(1)
-    give_back(0, *cell(0, 1))
-    cell(1, 0)
-    give_back(1, *cell(1, 1))
+    @pl.when(inner)
+    def _():
+        gather_core(2)
+        gather_core(3)
+        for g in range(2):
+            give_lent(g, *cell(zo, g, 1 - pair))
+        for g in range(2):
+            give_back(g, *cell(zb, g, 1 - pair, kept(g)))
 
     for d in order[::-1]:
         sb_copy(d).wait_recv()
     for zz in range(8):
         pltpu.make_async_copy(rt.at[zz], rt.at[zz], tb_r.at[zz]).wait()
+
+    @pl.when(outer)
+    def _():
+        for zz in range(8):
+            pltpu.make_async_copy(ro.at[zz], ro.at[zz], u_r.at[zz]).wait()
+
+    @pl.when(inner)
+    def _():
+        ro[...] = jnp.full((8, FR, LANES), NEG, BF16)
 
     own = act_ref[0, z * 4 + y] > 0
     halves = []
@@ -364,11 +454,14 @@
         la = unpack_lse(a)
         lb = jnp.where(own, unpack_lse(b), selfm[h, :, 0:1])
         b = jnp.where(own, b, sb[h, 0:64, :].astype(F32))
-        m = jnp.maximum(la, lb)
+        e = ro[h].astype(F32)
+        le = jnp.where(own, unpack_lse(e), NEG)
+        m = jnp.maximum(jnp.maximum(la, lb), le)
         wa = jnp.exp2((la - m) * LOG2E)
         wb = jnp.exp2((lb - m) * LOG2E)
-        inv = 1.0 / (wa + wb)
-        halves.append(a * (wa * inv) + b * (wb * inv))
+        we = jnp.exp2((le - m) * LOG2E)
+        inv = 1.0 / (wa + wb + we)
+        halves.append(a * (wa * inv) + b * (wb * inv) + e * (we * inv))
     pairs = [
         jnp.where(low, swap_halves(halves[2 * j]), halves[2 * j + 1]).astype(BF16) for j in range(4)
     ]
@@ -388,14 +481,22 @@
             tb_copy(zz).wait_send()
     for g in range(2):
         send_near(g).wait_send()
-        send_far(g).wait_send()
-        for i, p in enumerate((y,) + peers):
-            c_copy(i, p, g).wait_send()
-
-        @pl.when(inner)
-        def _():
-            for i in (1, 2):
-                onward(i, g).wait_send()
+        c_copy(0, g).wait_send()
+        c_copy(1, g).wait_send()
+
+    @pl.when(outer)
+    def _():
+        lend_queries().wait_send()
+
+    @pl.when(inner)
+    def _():
+        for g in range(2):
+            send_far(g).wait_send()
+            onward(g).wait_send()
+            c_copy(2, g).wait_send()
+            c_copy(3, g).wait_send()
+        for zz in range(8):
+            tu_copy(zz).wait_send()
 
 
 def body(hidden, control_ids, control_table, activity, ada, w_qkv, w_out):
@@ -406,15 +507,22 @@
         kernel,
         name="attention_block",
         out_shape=jax.ShapeDtypeStruct((FR, 1024), BF16),
-        in_specs=[vmem, vmem, vmem, pl.BlockSpec(memory_space=pltpu.SMEM), vmem, anywhere, anywhere],
+        in_specs=[anywhere] * 7,
         out_specs=vmem,
         scratch_shapes=[
+            pltpu.VMEM((FR, 1024), BF16),
+            pltpu.VMEM((1, FR), jnp.int32),
+            pltpu.VMEM((128, 1024), BF16),
+            pltpu.SMEM((1, 32), jnp.int32),
+            pltpu.VMEM((24, LANES), F32),
             pltpu.VMEM((3, 1024, 512), BF16),
             pltpu.VMEM((512, 1024), BF16),
             pltpu.VMEM((FR, 1024), F32),
             pltpu.VMEM((8, 96, LANES), BF16),
             pltpu.VMEM((4, 2, 512, LANES), BF16),
             pltpu.VMEM((8, 32, LANES), BF16),
+            pltpu.VMEM((8, 32, LANES), BF16),
+            pltpu.VMEM((512, LANES), BF16),
             pltpu.VMEM((512, LANES), BF16),
             pltpu.VMEM((8, 96, LANES), BF16),
             pltpu.VMEM((2, HALF, 8 * HALF), F32),
@@ -426,9 +534,12 @@
             pltpu.VMEM((8, FR, LANES), BF16),
             pltpu.VMEM((8, FR, LANES), BF16),
             pltpu.VMEM((8, FR, LANES), BF16),
+            pltpu.VMEM((8, FR, LANES), BF16),
+            pltpu.VMEM((8, FR, LANES), BF16),
+            dma((5,)),
             dma((4,)),
             dma((8,)), dma((8,)), dma((8,)), dma((8,)), dma((8,)), dma((8,)),
-            dma((4,)), dma((6,)), dma((4,)), dma((8,)), dma((8,)),
+            dma((4,)), dma((6,)), dma((2,)), dma((8,)), dma((8,)), dma, dma, dma((8,)), dma((8,)),
             dma((8,)), dma((8,)), dma((8,)), dma((8,)),
         ],
         compiler_params=pltpu.CompilerParams(

time: 46.9 us -> 42.8 us (0.913)
  Pallas kernels: 45.2 us -> 41.1 us
    pallas_call x1, Pallas kernels: 45.2 us -> 41.1 us  [body(): pl.pallas_call(kernel, name='attention_block', out_shape=jax.ShapeDtypeSt...]
where the time goes in v3:
time: 42.8 us; the launch traced here: 42.6 us
  Pallas kernels  41.1 us (96%)
  local copies, waits for them, and re-layouts  1.57 us (4%)
    pallas_call x1, Pallas kernels, body(): pl.pallas_call(kernel, name='attention_block', out_shape=jax.ShapeDtypeSt...  41.1 us
    unnamed x1, local copies, waits for them, and re-layouts  1.57 us

profile of v3, /device:TPU:1, one launch (start us, length us, event | category | flops | bytes accessed | tf_op | source)
XLA Modules:
  0.0 42.6 jit_solution(11518087117035151837)
XLA Ops:
  0.0 41.1 %attention_block.1 = bf16[64,1024]{1,0:T(8,128)(2,1)} custom-call(bf16[64,1024]{1,0:T(8,128)(2,1)} %bitcast.5, s32[1,64]{1,0:T(1,128)} %bitcast.7, bf16[128,1024]{1,0:T(8,128)(2,1)} %table_hbm.1, s32[1,32]{1,0:T(1,128)} %act_hbm.1, f32[24,128]{1,0:T(8,128)} %bitcast.6, bf16[1024,1536]{1,0:T(8,128)(2,1)} %wqkv_hbm.1, bf16[512,1024]{1,0:T(8,128)(2,1)} %wout_hbm.1), custom_call_target="tpu_custom_call" | custom-call | tf_op jit(solution)/shard_map/attention_block/pallas_call | solution.py:506
  41.1 1.6 %copy.9 = bf16[1,64,1024]{2,1,0:T(8,128)(2,1)} copy(bf16[1,64,1024]{2,1,0:T(8,128)(2,1)} %bitcast.4) | data formatting | bytes 262144

commit v4 on v3

--- a/solution.py
+++ b/solution.py
@@ -191,8 +191,12 @@
         sb[2 * j + 1, 64:96, :] = jnp.where(low32, swap_halves(a), b).astype(BF16)
     for d in order:
         zq_copy(d).start()
+
+    early = z < 4
+
     for d in order:
         st_copy(d).start()
+
 
     own_kv = pltpu.make_async_copy(
         sb.at[z, pl.ds(0, 64)], kvb.at[y, c, pl.ds(pl.multiple_of(z * 64, 64), 64)], zk_r.at[z]
@@ -358,6 +362,34 @@
             def _():
                 pltpu.make_async_copy(ob.at[zz], rt.at[zz], tb_r.at[zz]).start()
 
+    def sb_copy(d):
+        return pltpu.make_async_remote_copy(
+            src_ref=so.at[speer(d)], dst_ref=rs.at[s],
+            send_sem=sb_s.at[d], recv_sem=sb_r.at[d],
+            device_id=(speer(d), t), device_id_type=MESH,
+        )
+
+    def across_stems():
+        for d in order[::-1]:
+            st_copy(d).wait_recv()
+        row = lax.broadcasted_iota(jnp.int32, (LANES, LANES), 0)
+        col = lax.broadcasted_iota(jnp.int32, (LANES, LANES), 1)
+        keep = jnp.logical_and(jnp.bitwise_and(row, 15) == jnp.bitwise_and(col, 15), row != col)
+        for f0 in range(0, FR, 16):
+            q0 = 64 + f0 % 32
+            folded = jnp.concatenate([rst[ss, q0 : q0 + 16, :] for ss in range(8)], axis=0).astype(F32)
+            qst = unfold_low(folded) if f0 < 32 else unfold_high(folded)
+            kvst = jnp.concatenate([rst[ss, f0 : f0 + 16, :] for ss in range(8)], axis=0)
+            sc = jnp.where(keep, nt_dot(qst, kvst), NEG)
+            top = jnp.max(sc, axis=1, keepdims=True)
+            p = jnp.exp2((sc - top) * LOG2E).astype(BF16)
+            done = pack_part(top, jnp.dot(p, ones_values(kvst), preferred_element_type=F32))
+            for ss in range(8):
+                so[ss, f0 : f0 + 16, :] = done[16 * ss : 16 * ss + 16, :]
+        for d in order:
+            sb_copy(d).start()
+        rs[s] = so[s]
+
     gather_z(0)
     gather_z(1)
     for zz in range(8):
@@ -371,12 +403,17 @@
     for g in range(2):
         gather_near(g)
 
+
     @pl.when(inner)
     def _():
         for g in range(2):
             gather_far(2, g)
         lend_queries().wait_recv()
         unfold(qo, zo)
+
+    @pl.when(early)
+    def _():
+        across_stems()
 
     gather_core(0)
     gather_core(1)
@@ -395,42 +432,17 @@
         for g in range(2):
             gather_far(3, g)
 
-    for d in order[::-1]:
-        st_copy(d).wait_recv()
-    row = lax.broadcasted_iota(jnp.int32, (LANES, LANES), 0)
-    col = lax.broadcasted_iota(jnp.int32, (LANES, LANES), 1)
-    keep = jnp.logical_and(jnp.bitwise_and(row, 15) == jnp.bitwise_and(col, 15), row != col)
-    for f0 in range(0, FR, 16):
-        q0 = 64 + f0 % 32
-        folded = jnp.concatenate([rst[ss, q0 : q0 + 16, :] for ss in range(8)], axis=0).astype(F32)
-        qst = unfold_low(folded) if f0 < 32 else unfold_high(folded)
-        kvst = jnp.concatenate([rst[ss, f0 : f0 + 16, :] for ss in range(8)], axis=0)
-        sc = jnp.where(keep, nt_dot(qst, kvst), NEG)
-        top = jnp.max(sc, axis=1, keepdims=True)
-        p = jnp.exp2((sc - top) * LOG2E).astype(BF16)
-        done = pack_part(top, jnp.dot(p, ones_values(kvst), preferred_element_type=F32))
-        for ss in range(8):
-            so[ss, f0 : f0 + 16, :] = done[16 * ss : 16 * ss + 16, :]
-
-    def sb_copy(d):
-        return pltpu.make_async_remote_copy(
-            src_ref=so.at[speer(d)], dst_ref=rs.at[s],
-            send_sem=sb_s.at[d], recv_sem=sb_r.at[d],
-            device_id=(speer(d), t), device_id_type=MESH,
-        )
-
-    for d in order:
-        sb_copy(d).start()
-    rs[s] = so[s]
-
     @pl.when(inner)
     def _():
         gather_core(2)
         gather_core(3)
         for g in range(2):
             give_lent(g, *cell(zo, g, 1 - pair))
-        for g in range(2):
             give_back(g, *cell(zb, g, 1 - pair, kept(g)))
+
+    @pl.when(jnp.logical_not(early))
+    def _():
+        across_stems()
 
     for d in order[::-1]:
         sb_copy(d).wait_recv()

time: 42.8 us -> 41.2 us (0.963)
  Pallas kernels: 41.1 us -> 39.5 us
    pallas_call x1, Pallas kernels: 41.1 us -> 39.5 us  [body(): pl.pallas_call(kernel, name='attention_block', out_shape=jax.ShapeDtypeSt...]
where the time goes in v4:
time: 41.2 us; the launch traced here: 41.1 us
  Pallas kernels  39.5 us (96%)
  local copies, waits for them, and re-layouts  1.57 us (4%)
    pallas_call x1, Pallas kernels, body(): pl.pallas_call(kernel, name='attention_block', out_shape=jax.ShapeDtypeSt...  39.5 us
    unnamed x1, local copies, waits for them, and re-layouts  1.57 us

profile of v4, /device:TPU:1, one launch (start us, length us, event | category | flops | bytes accessed | tf_op | source)
XLA Modules:
  0.0 41.1 jit_solution(5277771610955908765)
XLA Ops:
  0.0 39.5 %attention_block.1 = bf16[64,1024]{1,0:T(8,128)(2,1)} custom-call(bf16[64,1024]{1,0:T(8,128)(2,1)} %bitcast.5, s32[1,64]{1,0:T(1,128)} %bitcast.7, bf16[128,1024]{1,0:T(8,128)(2,1)} %table_hbm.1, s32[1,32]{1,0:T(1,128)} %act_hbm.1, f32[24,128]{1,0:T(8,128)} %bitcast.6, bf16[1024,1536]{1,0:T(8,128)(2,1)} %wqkv_hbm.1, bf16[512,1024]{1,0:T(8,128)(2,1)} %wout_hbm.1), custom_call_target="tpu_custom_call" | custom-call | tf_op jit(solution)/shard_map/attention_block/pallas_call | solution.py:518
  39.5 1.6 %copy.9 = bf16[1,64,1024]{2,1,0:T(8,128)(2,1)} copy(bf16[1,64,1024]{2,1,0:T(8,128)(2,1)} %bitcast.4) | data formatting | bytes 262144

commit v5 on v4

--- a/solution.py
+++ b/solution.py
@@ -408,8 +408,6 @@
     def _():
         for g in range(2):
             gather_far(2, g)
-        lend_queries().wait_recv()
-        unfold(qo, zo)
 
     @pl.when(early)
     def _():
@@ -434,6 +432,8 @@
 
     @pl.when(inner)
     def _():
+        lend_queries().wait_recv()
+        unfold(qo, zo)
         gather_core(2)
         gather_core(3)
         for g in range(2):

time: 41.2 us -> 40.8 us (level)
  Pallas kernels: 39.5 us -> 38.7 us
    pallas_call x1, Pallas kernels: 39.5 us -> 38.7 us  [body(): pl.pallas_call(kernel, name='attention_block', out_shape=jax.ShapeDtypeSt...]
where the time goes in v5:
time: 40.8 us; the launch traced here: 40.3 us
  Pallas kernels  38.7 us (95%)
  local copies, waits for them, and re-layouts  1.57 us (4%)
    pallas_call x1, Pallas kernels, body(): pl.pallas_call(kernel, name='attention_block', out_shape=jax.ShapeDtypeSt...  38.7 us
    unnamed x1, local copies, waits for them, and re-layouts  1.57 us

profile of v5, /device:TPU:1, one launch (start us, length us, event | category | flops | bytes accessed | tf_op | source)
XLA Modules:
  0.0 40.3 jit_solution(17031701527818868164)
XLA Ops:
  0.0 38.7 %attention_block.1 = bf16[64,1024]{1,0:T(8,128)(2,1)} custom-call(bf16[64,1024]{1,0:T(8,128)(2,1)} %bitcast.5, s32[1,64]{1,0:T(1,128)} %bitcast.7, bf16[128,1024]{1,0:T(8,128)(2,1)} %table_hbm.1, s32[1,32]{1,0:T(1,128)} %act_hbm.1, f32[24,128]{1,0:T(8,128)} %bitcast.6, bf16[1024,1536]{1,0:T(8,128)(2,1)} %wqkv_hbm.1, bf16[512,1024]{1,0:T(8,128)(2,1)} %wout_hbm.1), custom_call_target="tpu_custom_call" | custom-call | tf_op jit(solution)/shard_map/attention_block/pallas_call | solution.py:518
  38.7 1.6 %copy.9 = bf16[1,64,1024]{2,1,0:T(8,128)(2,1)} copy(bf16[1,64,1024]{2,1,0:T(8,128)(2,1)} %bitcast.4) | data formatting | bytes 262144
